TPU v7x, 128 devices: a whole 4x4x4 slice. The times are simulated.
128 devices in a mesh: dp: 16 (over x, z), tensor: 8 (over y, core).
Axes of the slice: x: 4, y: 4, z: 4, core: 2. Of those that a mesh axis runs over, the one named last changes fastest.
Arguments:
- x_seq: bfloat16 [8192, 8192], P(('dp', 'tensor')), may hold values from -0.0625 to 0.0625
- grad_out: bfloat16 [8192, 14336], P('dp', 'tensor'), may hold values from -6 to 6
- w_tiles: bfloat16 [2560, 128, 128], P('tensor'), may hold values from -0.09375 to 0.09375
- block_rows: int32 [8, 320], P('tensor'), may hold values from 0 to 63, as said below
- block_cols: int32 [8, 320], P('tensor'), may hold values from 0 to 13
- counts: int32 [8], P('tensor'), may hold values from 80 to 320, as said below
- owner: int32 [8, 320], P('tensor'), may hold values from 0 to 319, as said below
Outputs:
- grad_in: bfloat16 [8192, 8192], P(('dp', 'tensor'))
- dw_owned: float32 [8, 320, 128, 128], P('tensor', 'dp')
Inputs may be any that keep to these rules, and one draw needn't show every extreme that they name: Slot k of tensor shard s keeps the block at block row block_rows[s, k] and block column block_cols[s, k]; among the first counts[s] slots of a shard no two name the same block. `counts`: some shard uses all 320 slots. `owner`: each row is a permutation of 0 to 319.
All inputs are finite; a program needn't handle non-finite values.
Results may differ from a plain program's by a relative error of at most 0.018.
Values may be sent and summed in bfloat16 or wider, within the bound.
A program may use at most 256 MiB of HBM per device.

v0:
```python
import jax
import jax.numpy as jnp
from jax import lax
from jax.experimental import pallas as pl
from jax.experimental.pallas import tpu as pltpu
from jax.sharding import PartitionSpec as P

MESH = pl.DeviceIdType.MESH
RING = 4
TILE = 128
OWNERS = RING * RING
NCOPY = 80
COL_CHUNKS = 4
COL_STEP = 256
UNROLLS = (8, 4, 2, 1)


def pieces_of(per_owner):
    half = per_owner // 2
    late = half * 2 // 5
    return (half - late, late)


def fill_tables(rows_ref, cols_ref, owner_ref, counts, lut_v, col_blocks, blocks):
    slots = owner_ref.shape[1]
    per_owner = slots // OWNERS
    half = per_owner // 2
    early, late = pieces_of(per_owner)
    slot = lax.broadcasted_iota(jnp.int32, (1, slots), 1)
    live = (slot < counts[0]).astype(jnp.int32)

    def quotient(a, n, limit):
        return sum((a >= n * m).astype(jnp.int32) for m in range(1, limit))

    at = owner_ref[...]
    chip = quotient(at, per_owner, OWNERS)
    at = at - chip * per_owner
    x = quotient(chip, RING, RING)
    z = chip - x * RING
    h = (at >= half).astype(jnp.int32)
    at = at - h * half
    i = (at >= early).astype(jnp.int32)
    at = at - i * early
    u, v = x + h * (z - x), z + h * (x - z)
    place = (h * half + i * early) * OWNERS + (u * RING + v) * (early + i * (late - early)) + at
    code = rows_ref[...] * 16 + col_blocks + live * (cols_ref[...] - col_blocks)
    key = live * (rows_ref[...] * col_blocks + cols_ref[...] + 1) - 1

    places, tables = pl.cdiv(slots, TILE), pl.cdiv(blocks, TILE)
    totals = [jnp.zeros((1, TILE), jnp.int32) for _ in range(places + tables)]
    for first in range(0, slots, TILE):
        n = min(TILE, slots - first)

        def upright(a, first=first, n=n):
            return jnp.broadcast_to(a[:, first : first + n], (TILE, n)).T

        lane = lax.broadcasted_iota(jnp.int32, (n, TILE), 1)
        index = lax.broadcasted_iota(jnp.int32, (n, TILE), 0) + (first - slots)
        place_n, code_n, key_n = upright(place), upright(code), upright(key)
        for m in range(places + tables):
            wanted, had, value = (
                (lane + m * TILE, place_n, code_n) if m < places else (lane + (m - places) * TILE, key_n, index)
            )
            match = (had == wanted).astype(jnp.int32)
            if m < places:
                totals[m] = jnp.maximum(totals[m], jnp.max(match * value, axis=0, keepdims=True))
            else:
                totals[m] = jnp.minimum(totals[m], jnp.min(match * value, axis=0, keepdims=True))
    lut_v[...] = jnp.zeros_like(lut_v)
    for m, total in enumerate(totals):
        lut_v[m : m + 1, :] = total


def kernel(
    rows_ref, cols_ref, owner_ref, counts, x_ref, g_hbm, w_hbm, gi_ref, dw_ref,
    xg, part, pr, g, gt, buf, yr1, yr2, e1, e2, e3, e4, l1, l2, l3, l4, lut_v, lut_s, lsem, ssem, rsem,
):
    rows, width = x_ref.shape
    tokens, shard_width = g_hbm.shape
    slots = w_hbm.shape[0]
    col_blocks = shard_width // TILE
    per_owner = slots // OWNERS
    hrows = rows // 2
    top, bottom = pl.ds(0, hrows), pl.ds(hrows, hrows)
    quarters = [pl.ds(i * (rows // 4), rows // 4) for i in range(4)]

    p = lax.axis_index("dp")
    s = lax.axis_index("tensor")
    x, z = p // RING, p % RING
    y, q = s // 2, s % 2
    yu, yd, yo = (y + 1) % RING, (y + 3) % RING, (y + 2) % RING
    other = 1 - q

    def at_y(row, core):
        return (p, row * 2 + core)

    def at_x(pos):
        return (pos * RING + z, s)

    def at_z(pos):
        return (x * RING + pos, s)

    started = []

    def send(src, dst, device):
        i = len(started)
        copy = pltpu.make_async_remote_copy(
            src_ref=src, dst_ref=dst, send_sem=ssem.at[i], recv_sem=rsem.at[i],
            device_id=device, device_id_type=MESH,
        )
        copy.start()
        started.append(copy)
        return copy

    left = []

    def sent(copy):
        copy.wait_send()
        left.append(copy)

    up, down, across = at_y(yu, q), at_y(yd, q), at_y(y, other)

    load_x = pltpu.make_async_copy(x_ref, xg.at[s], lsem.at[0])
    load_g = pltpu.make_async_copy(g_hbm, g, lsem.at[1])
    load_w = pltpu.make_async_copy(w_hbm, buf.at[pl.ds(0, slots)], lsem.at[2])
    load_x.start()

    barrier = pltpu.get_barrier_semaphore()
    peers = [
        up, down, across,
        at_x((x + 1) % RING), at_x((x + 3) % RING), at_z((z + 1) % RING), at_z((z + 3) % RING),
    ]
    for peer in peers:
        pl.semaphore_signal(barrier, inc=1, device_id=peer, device_id_type=MESH)
    load_x.wait()
    pl.semaphore_wait(barrier, len(peers))

    up_top = send(xg.at[s, top], xg.at[s, top], up)
    down_bottom = send(xg.at[s, bottom], xg.at[s, bottom], down)
    up_bottom = send(xg.at[s, bottom], xg.at[s, bottom], up)
    down_top = send(xg.at[s, top], xg.at[s, top], down)
    sib_own = send(xg.at[s], xg.at[s], across)

    load_g.start()
    load_w.start()
    fill_tables(rows_ref, cols_ref, owner_ref, counts, lut_v, col_blocks, width // TILE * col_blocks)
    load_lut = pltpu.make_async_copy(lut_v, lut_s, lsem.at[3])
    load_lut.start()
    load_g.wait()
    for c in range(col_blocks):
        gt[c] = g[:, c * TILE : (c + 1) * TILE].T
    gt[col_blocks] = jnp.zeros((TILE, tokens), gt.dtype)
    buf[slots] = jnp.zeros((TILE, TILE), buf.dtype)
    load_w.wait()
    load_lut.wait()

    table_at = pl.cdiv(slots, TILE) * TILE

    def lut(i):
        return lut_s[lax.div(i, TILE), lax.rem(i, TILE)]

    cols_per_chunk = width // COL_CHUNKS
    blocks = COL_STEP // TILE

    def part_chunk(n):
        def body(i, carry):
            first = n * cols_per_chunk + i * COL_STEP
            first_block = n * (cols_per_chunk // TILE) + i * blocks
            weight = jnp.concatenate(
                [
                    jnp.concatenate(
                        [buf[lut(table_at + (first_block + b) * col_blocks + c) + slots] for c in range(col_blocks)], axis=1
                    )
                    for b in range(blocks)
                ],
                axis=0,
            )
            product = lax.dot_general(
                g[...], weight, (((1,), (1,)), ((), ())), preferred_element_type=jnp.float32
            )
            product = product.astype(jnp.bfloat16).reshape(RING, 2, rows, COL_STEP)
            columns = pl.ds(pl.multiple_of(first, COL_STEP), COL_STEP)
            for core in range(2):
                part[core, :, :, columns] = product[:, core]
            return carry

        lax.fori_loop(0, cols_per_chunk // COL_STEP, body, 0)
        columns = pl.ds(n * cols_per_chunk, cols_per_chunk)
        return send(part.at[other, :, :, columns], pr.at[:, :, columns], across)

    pair = [part_chunk(0), part_chunk(1)]
    up_top.wait_recv()
    from_down, from_up, from_far = yd * 2 + q, yu * 2 + q, yo * 2 + q
    fwd_up = [send(xg.at[from_down, at], xg.at[from_down, at], up) for at in quarters[:2]]
    down_bottom.wait_recv()
    fwd_down = [send(xg.at[from_up, at], xg.at[from_up, at], down) for at in quarters[2:]]
    pair += [part_chunk(2), part_chunk(3)]
    up_bottom.wait_recv()
    sib_down = send(xg.at[from_down], xg.at[from_down], across)
    down_top.wait_recv()
    sib_up = send(xg.at[from_up], xg.at[from_up], across)

    for copy in pair:
        copy.wait_recv()
    row_step = 16
    steps = rows // row_step

    def add_pair(i, carry):
        at = pl.ds(pl.multiple_of((i % steps) * row_step, row_step), row_step)
        row = i // steps
        total = part[q, row, at].astype(jnp.float32) + pr[row, at].astype(jnp.float32)
        part[q, row, at] = total.astype(jnp.bfloat16)
        return carry

    lax.fori_loop(0, RING * steps, add_pair, 0)

    sib_far = []
    for i in range(2):
        for copy, at in ((fwd_up[i], quarters[i]), (fwd_down[i], quarters[i + 2])):
            copy.wait_recv()
            sib_far.append(send(xg.at[from_far, at], xg.at[from_far, at], across))

    gi_up_far = send(part.at[q, yo, top], yr1.at[0], up)
    gi_down_far = send(part.at[q, yo, bottom], yr1.at[1], down)
    gi_up_near = send(part.at[q, yu, bottom], yr2.at[0, bottom], up)
    gi_down_near = send(part.at[q, yd, top], yr2.at[1, top], down)

    for copy in (sib_own, sib_down, sib_up, *sib_far):
        copy.wait_recv()

    def tile_grads(first, count):
        unroll = next(n for n in UNROLLS if count % n == 0)

        def body(i, carry):
            for k in range(unroll):
                j = first + i * unroll + k
                code = lut(j)
                rhs = xg[:, :, pl.ds(lax.div(code, 16) * TILE, TILE)].reshape(tokens, TILE)
                grad = jnp.dot(gt[lax.rem(code, 16)], rhs, preferred_element_type=jnp.float32)
                buf[j] = grad.astype(jnp.bfloat16)
            return carry

        lax.fori_loop(0, count // unroll, body, 0)

    def piece_of(h, i):
        u, v, at_u, at_v = (x, z, at_x, at_z) if h == 0 else (z, x, at_z, at_x)
        split = pieces_of(per_owner)
        group = split[i]
        chunk = RING * group
        slot = h * (per_owner // 2) + sum(split[:i])
        first = slot * OWNERS
        uu, ud, uo = (u + 1) % RING, (u + 3) % RING, (u + 2) % RING
        return dict(
            n=h, v=v, to_uu=at_u(uu), to_ud=at_u(ud), vu=(v + 1) % RING, vd=(v + 3) % RING,
            vo=(v + 2) % RING, at_v=at_v, far=first + uo * chunk, next=first + uu * chunk,
            prev=first + ud * chunk, own=first + u * chunk, group=group, hc=chunk // 2, slot=slot,
            d=((e1, e2, e3, e4), (l1, l2, l3, l4))[i], out=([], []),
        )

    low, high = pl.ds(0, TILE // 2), pl.ds(TILE // 2, TILE // 2)

    def some(first, count):
        return buf.at[pl.ds(first, count)]

    def far_out(pieces, first, count):
        for f in pieces:
            n, hc, d1 = f["n"], f["hc"], f["d"][0]
            for side, to in enumerate((f["to_uu"], f["to_ud"])):
                at = f["far"] + side * hc + first
                tile_grads(at, count)
                f["out"][side].append(send(some(at, count), d1.at[n, side, pl.ds(first, count)], to))

    def near_tiles(f):
        tile_grads(f["next"], 2 * f["hc"])
        tile_grads(f["prev"], 2 * f["hc"])

    def near_out(f):
        n, hc, d2 = f["n"], f["hc"], f["d"][1]
        f["near_u"] = send(some(f["next"] + hc, hc), d2.at[n, 0, pl.ds(hc, hc)], f["to_uu"])
        f["near_d"] = send(some(f["prev"], hc), d2.at[n, 1, pl.ds(0, hc)], f["to_ud"])

    def add_far(f, dst, side):
        d1 = f["d"][0]

        def body(i, carry):
            total = buf[dst + i].astype(jnp.float32) + d1[f["n"], side, i].astype(jnp.float32)
            buf[dst + i] = total.astype(jnp.bfloat16)
            return carry

        lax.fori_loop(0, f["hc"], body, 0)

    def sums_out(f):
        n, hc, d2 = f["n"], f["hc"], f["d"][1]
        for copy in f["out"][0]:
            copy.wait_recv()
        add_far(f, f["next"], 0)
        f["sum_u"] = send(some(f["next"], hc), d2.at[n, 0, pl.ds(0, hc)], f["to_uu"])
        for copy in f["out"][1]:
            copy.wait_recv()
        add_far(f, f["prev"] + hc, 1)
        f["sum_d"] = send(some(f["prev"] + hc, hc), d2.at[n, 1, pl.ds(hc, hc)], f["to_ud"])

    def settle(f, pos):
        n, group, d2 = f["n"], f["group"], f["d"][1]
        lead = pos * group

        def body(i, carry):
            total = buf[f["own"] + lead + i].astype(jnp.float32)
            total = total + d2[n, 0, lead + i].astype(jnp.float32)
            total = total + d2[n, 1, lead + i].astype(jnp.float32)
            buf[f["own"] + lead + i] = total.astype(jnp.bfloat16)
            return carry

        lax.fori_loop(0, group, body, 0)
        return pl.ds(f["own"] + lead, group)

    def second_out(f):
        n, group, (_, _, d3, d4) = f["n"], f["group"], f["d"]
        to_vu, to_vd = f["at_v"](f["vu"]), f["at_v"](f["vd"])
        for name in ("near_u", "near_d", "sum_u", "sum_d"):
            f[name].wait_recv()
        far = settle(f, f["vo"])
        f["far_u2"] = send(buf.at[far, low], d3.at[n, 0], to_vu)
        f["far_d2"] = send(buf.at[far, high], d3.at[n, 1], to_vd)
        following = settle(f, f["vu"])
        f["near_u2"] = send(buf.at[following, high], d4.at[n, 0, :, high], to_vu)
        preceding = settle(f, f["vd"])
        f["near_d2"] = send(buf.at[preceding, low], d4.at[n, 1, :, low], to_vd)
        settle(f, f["v"])

    def second_sums(f):
        n, group, (_, _, d3, d4) = f["n"], f["group"], f["d"]
        to_vu, to_vd = f["at_v"](f["vu"]), f["at_v"](f["vd"])
        for name, side, pos, half, dev in (("u", 0, "vu", low, to_vu), ("d", 1, "vd", high, to_vd)):
            f[f"far_{name}2"].wait_recv()
            dst = f["own"] + f[pos] * group

            def body(i, carry, dst=dst, half=half, side=side):
                total = buf[dst + i, half].astype(jnp.float32) + d3[n, side, i].astype(jnp.float32)
                buf[dst + i, half] = total.astype(jnp.bfloat16)
                return carry

            lax.fori_loop(0, group, body, 0)
            f[f"sum_{name}2"] = send(buf.at[pl.ds(dst, group), half], d4.at[n, side, :, half], dev)

    def finish(f):
        n, group, d4 = f["n"], f["group"], f["d"][3]
        for name in ("near_u2", "near_d2", "sum_u2", "sum_d2"):
            f[name].wait_recv()

        def body(i, carry):
            total = buf[f["own"] + f["v"] * group + i].astype(jnp.float32)
            total = total + d4[n, 0, i].astype(jnp.float32) + d4[n, 1, i].astype(jnp.float32)
            dw_ref[f["slot"] + i] = total.T
            return carry

        lax.fori_loop(0, group, body, 0)

    def add_rows(row, first, term):
        def body(i, carry):
            at = pl.ds(pl.multiple_of(i * row_step, row_step), row_step)
            to = pl.ds(pl.multiple_of(first + i * row_step, row_step), row_step)
            total = part[q, row, to].astype(jnp.float32) + yr1[term, at].astype(jnp.float32)
            part[q, row, to] = total.astype(jnp.bfloat16)
            return carry

        lax.fori_loop(0, hrows // row_step, body, 0)

    early = [piece_of(0, 0), piece_of(1, 0)]
    late = [piece_of(0, 1), piece_of(1, 1)]
    lead = 4
    far_out(early, 0, lead)
    far_out(early, lead, early[0]["hc"] - lead)
    far_out(late, 0, late[0]["hc"])
    for f in early:
        near_tiles(f)
    for f in early:
        sums_out(f)
    for f in early:
        near_out(f)
    for f in late:
        near_tiles(f)
    for f in early + late:
        tile_grads(f["own"], 2 * f["hc"])

    gi_up_far.wait_recv()
    add_rows(yu, 0, 0)
    gi_up_sum = send(part.at[q, yu, top], yr2.at[0, top], up)
    gi_down_far.wait_recv()
    add_rows(yd, hrows, 1)
    gi_down_sum = send(part.at[q, yd, bottom], yr2.at[1, bottom], down)

    for f in early:
        sent(f["sum_u"])
        sent(f["sum_d"])
    for f in late:
        sums_out(f)
    for f in early:
        sent(f["near_u"])
        sent(f["near_d"])
    for f in late:
        near_out(f)
    for f in early:
        second_out(f)
    for f in early:
        second_sums(f)
    for f in late:
        second_out(f)
    for copy in (gi_up_near, gi_down_near, gi_up_sum, gi_down_sum):
        copy.wait_recv()
    for f in late:
        second_sums(f)

    def finish_rows(i, carry):
        at = pl.ds(pl.multiple_of(i * row_step, row_step), row_step)
        total = part[q, y, at].astype(jnp.float32) + yr2[0, at].astype(jnp.float32)
        gi_ref[at, :] = (total + yr2[1, at].astype(jnp.float32)).astype(jnp.bfloat16)
        return carry

    lax.fori_loop(0, steps, finish_rows, 0)
    for f in early + late:
        finish(f)
    for copy in started:
        if all(copy is not gone for gone in left):
            copy.wait_send()


def per_device(x_seq, grad_out, w_tiles, block_rows, block_cols, counts, owner):
    rows, width = x_seq.shape
    tokens, shard_width = grad_out.shape
    slots = w_tiles.shape[0]
    col_blocks = shard_width // TILE
    per_owner = slots // OWNERS
    split = pieces_of(per_owner)
    lut_rows = pl.cdiv(pl.cdiv(slots, TILE) + pl.cdiv(width // TILE * col_blocks, TILE), 8) * 8

    bf16 = jnp.bfloat16
    any_space = pl.BlockSpec(memory_space=pl.ANY)
    smem = pl.BlockSpec(memory_space=pltpu.SMEM)
    vmem = pl.BlockSpec(memory_space=pltpu.VMEM)
    grad_in, owned = pl.pallas_call(
        kernel,
        out_shape=(
            pltpu.VMEM((rows, width), bf16),
            pltpu.VMEM((per_owner, TILE, TILE), jnp.float32),
        ),
        in_specs=[vmem, vmem, vmem, smem, any_space, any_space, any_space],
        out_specs=(vmem, vmem),
        scratch_shapes=[
            pltpu.VMEM((2 * RING, rows, width), bf16),
            pltpu.VMEM((2, RING, rows, width), bf16),
            pltpu.VMEM((RING, rows, width), bf16),
            pltpu.VMEM((tokens, shard_width), bf16),
            pltpu.VMEM((col_blocks + 1, TILE, tokens), bf16),
            pltpu.VMEM((slots + 1, TILE, TILE), bf16),
            pltpu.VMEM((2, rows // 2, width), bf16),
            pltpu.VMEM((2, rows, width), bf16),
            *[
                pltpu.VMEM((2, 2, *shape, TILE), bf16)
                for n in split
                for shape in ((2 * n, TILE), (4 * n, TILE), (n, TILE // 2), (n, TILE))
            ],
            pltpu.VMEM((lut_rows, TILE), jnp.int32),
            pltpu.SMEM((lut_rows, TILE), jnp.int32),
            pltpu.SemaphoreType.DMA((4,)),
            pltpu.SemaphoreType.DMA((NCOPY,)),
            pltpu.SemaphoreType.DMA((NCOPY,)),
        ],
        compiler_params=pltpu.CompilerParams(
            collective_id=0, has_side_effects=True, vmem_limit_bytes=60 * 1024 * 1024
        ),
        cost_estimate=pl.CostEstimate(
            flops=2 * tokens * shard_width * width + 2 * slots * tokens * TILE * TILE,
            bytes_accessed=2 * (slots * TILE * TILE + tokens * shard_width + 2 * rows * width)
            + 4 * per_owner * TILE * TILE,
            transcendentals=0,
        ),
    )(block_rows, block_cols, owner, counts, x_seq, grad_out, w_tiles)
    return grad_in, owned.reshape(1, per_owner, TILE, TILE)


def solution(mesh):
    return jax.shard_map(
        per_device,
        mesh=mesh,
        in_specs=(
            P(("dp", "tensor"), None),
            P("dp", "tensor"),
            P("tensor", None, None),
            P("tensor", None),
            P("tensor", None),
            P("tensor"),
            P("tensor", None),
        ),
        out_specs=(P(("dp", "tensor"), None), P("tensor", "dp", None, None)),
        check_vma=False,
    )
```

profile of v0, /device:TPU:1, one launch (start us, length us, event | category | flops | bytes accessed | tf_op | source)
XLA Modules:
  0.0 108.1 jit_solution(13005737302557123353)
XLA Ops:
  1.3 104.7 %shard_map.86 = (bf16[64,8192]{1,0:T(8,128)(2,1)S(1)}, f32[20,128,128]{2,1,0:T(8,128)S(1)}) custom-call(s32[1,320]{1,0:T(1,128)} %rows_ref.1, s32[1,320]{1,0:T(1,128)} %cols_ref.1, s32[1,320]{1,0:T(1,128)} %owner_ref.1, s32[1]{0:T(128)S(6)} %copy.13.counts, bf16[64,8192]{1,0:T(8,128)(2,1)} %x_ref.1, bf16[512,1792]{1,0:T(8,128)(2,1)} %g_hbm.1, ...), custom_call_target="tpu_custom_call" | custom-call | flops 20401094656 | bytes 15728640 | tf_op jit(solution)/shard_map/pallas_call | solution.py:441
  106.0 1.0 copy.11
  107.0 1.1 copy.12
where the time goes:
time: 108 us
  Pallas kernels  105 us (97%)
  local copies, waits for them, and re-layouts  2.03 us (2%)
  between operations  1.29 us (1%)
    pallas_call x1, Pallas kernels, per_device(): pl.pallas_call(kernel, out_shape=(pltpu.VMEM((rows, width), bf16), pltpu....  105 us

commit v1 on v0

--- a/solution.py
+++ b/solution.py
@@ -71,6 +71,14 @@
         lut_v[m : m + 1, :] = total
 
 
+def copy_out(gi_in, dw_in, gi_out, dw_out, sem):
+    copies = [pltpu.make_async_copy(gi_in, gi_out, sem.at[0]), pltpu.make_async_copy(dw_in, dw_out, sem.at[1])]
+    for copy in copies:
+        copy.start()
+    for copy in copies:
+        copy.wait()
+
+
 def kernel(
     rows_ref, cols_ref, owner_ref, counts, x_ref, g_hbm, w_hbm, gi_ref, dw_ref,
     xg, part, pr, g, gt, buf, yr1, yr2, e1, e2, e3, e4, l1, l2, l3, l4, lut_v, lut_s, lsem, ssem, rsem,
@@ -132,13 +140,13 @@
     ]
     for peer in peers:
         pl.semaphore_signal(barrier, inc=1, device_id=peer, device_id_type=MESH)
+    pl.semaphore_wait(barrier, len(peers))
+
+    up_top = send(x_ref.at[top], xg.at[s, top], up)
+    down_bottom = send(x_ref.at[bottom], xg.at[s, bottom], down)
+    up_bottom = send(x_ref.at[bottom], xg.at[s, bottom], up)
+    down_top = send(x_ref.at[top], xg.at[s, top], down)
     load_x.wait()
-    pl.semaphore_wait(barrier, len(peers))
-
-    up_top = send(xg.at[s, top], xg.at[s, top], up)
-    down_bottom = send(xg.at[s, bottom], xg.at[s, bottom], down)
-    up_bottom = send(xg.at[s, bottom], xg.at[s, bottom], up)
-    down_top = send(xg.at[s, top], xg.at[s, top], down)
     sib_own = send(xg.at[s], xg.at[s], across)
 
     load_g.start()
@@ -476,6 +484,17 @@
             transcendentals=0,
         ),
     )(block_rows, block_cols, owner, counts, x_seq, grad_out, w_tiles)
+    grad_in, owned = pl.pallas_call(
+        copy_out,
+        out_shape=(
+            jax.ShapeDtypeStruct((rows, width), bf16),
+            jax.ShapeDtypeStruct((per_owner, TILE, TILE), jnp.float32),
+        ),
+        in_specs=[vmem, vmem],
+        out_specs=(any_space, any_space),
+        scratch_shapes=[pltpu.SemaphoreType.DMA((2,))],
+        compiler_params=pltpu.CompilerParams(vmem_limit_bytes=4 * 1024 * 1024),
+    )(grad_in, owned)
     return grad_in, owned.reshape(1, per_owner, TILE, TILE)
 
 

time: 108 us -> 107 us (level)
  local copies, waits for them, and re-layouts: 2.03 us -> 0 us
    unnamed x2 -> x0, local copies, waits for them, and re-layouts: 2.03 us -> none
    pallas_call x0 -> x1, Pallas kernels: none -> 1.42 us  [per_device(): pl.pallas_call(copy_out, out_shape=(jax.ShapeDtypeStruct((rows, width), b...]
where the time goes in v1:
time: 107 us
  Pallas kernels  105 us (98%)
  between operations  1.45 us (1%)
    pallas_call x1, Pallas kernels, per_device(): pl.pallas_call(kernel, out_shape=(pltpu.VMEM((rows, width), bf16), pltpu....  104 us

profile of v1, /device:TPU:1, one launch (start us, length us, event | category | flops | bytes accessed | tf_op | source)
XLA Modules:
  0.0 106.9 jit_solution(13169557050553174093)
XLA Ops:
  1.3 104.0 %shard_map.86 = (bf16[64,8192]{1,0:T(8,128)(2,1)S(1)}, f32[20,128,128]{2,1,0:T(8,128)S(1)}) custom-call(s32[1,320]{1,0:T(1,128)} %rows_ref.1, s32[1,320]{1,0:T(1,128)} %cols_ref.1, s32[1,320]{1,0:T(1,128)} %owner_ref.1, s32[1]{0:T(128)S(6)} %copy.9.counts, bf16[64,8192]{1,0:T(8,128)(2,1)} %x_ref.1, bf16[512,1792]{1,0:T(8,128)(2,1)} %g_hbm.1, ...), custom_call_target="tpu_custom_call" | custom-call | flops 20401094656 | bytes 15728640 | tf_op jit(solution)/shard_map/pallas_call | solution.py:449
  105.3 1.4 %shard_map.87 = (bf16[64,8192]{1,0:T(8,128)(2,1)}, f32[20,128,128]{2,1,0:T(8,128)}) custom-call(bf16[64,8192]{1,0:T(8,128)(2,1)S(1)} %get-tuple-element.6.gi_in, f32[20,128,128]{2,1,0:T(8,128)S(1)} %get-tuple-element.7.dw_in), custom_call_target="tpu_custom_call" | custom-call | tf_op jit(solution)/shard_map/pallas_call | solution.py:487
